TPU v7x, 32 devices: a whole 2x2x4 slice. The times are simulated.
32 devices in a mesh: blk: 16 (over z, y, x), grp: 2 (over core).
Axes of the slice: x: 2, y: 2, z: 4, core: 2. Of those that a mesh axis runs over, the one named last changes fastest.
Arguments:
- rhs: float32 [4, 16, 128, 128], P(None, 'blk', 'grp'), may hold values from -6 to 6
- diag_inv: bfloat16 [4, 16, 128, 128], P(None, 'blk'), as said below
- off_blocks: bfloat16 [3, 16, 4, 128, 128], P(None, 'blk'), may hold values from -0.25 to 0.25
- columns: int32 [3, 16, 4], P(None, 'blk'), may hold values from 0 to 47, as said below
- owner: int32 [4, 16], replicated, may hold values from 0 to 15, each once within a row
- train_desc: bfloat16 [4, 16, 128, 1024], P(None, 'blk'), may hold values from -6 to 6
- pred_desc: bfloat16 [2, 512, 1024], P('grp'), may hold values from -6 to 6
Outputs:
- solved: bfloat16 [4, 16, 128, 128], P(None, 'blk', 'grp')
- predicted: float32 [2, 512, 128], P('grp', 'blk')
Inputs may be any that keep to these rules, and one draw needn't show every extreme that they name: `columns`: the 4 numbers of a block row of level l (array index l - 1) are distinct block-row numbers of levels below l, that is below l * 16. Each row of owner is a permutation of the device indices along blk. `diag_inv`: each block is zero below its diagonal.
All inputs are finite; a program needn't handle non-finite values.
Results may differ from a plain program's by a relative error of at most 0.007.
Values may be sent and summed in bfloat16 or wider, within the bound.
A program may use at most 128 MiB of HBM per device.

v0:
```python
import jax
import jax.numpy as jnp
from jax import lax
from jax.sharding import PartitionSpec as P


def kernel_rows(queries, train_flat):
    feature_width = train_flat.shape[1]
    inner = lax.dot_general(
        queries, train_flat, (((1,), (1,)), ((), ())), preferred_element_type=jnp.float32
    )
    scaled = inner / feature_width
    return (scaled * scaled).astype(jnp.bfloat16)


def body(rhs, diag_inv, off_blocks, columns, owner, train_desc, pred_desc):
    levels = rhs.shape[0]
    panel_rows = rhs.shape[2]
    block_size = rhs.shape[3]
    level_size = lax.axis_size("blk")
    feature_width = train_desc.shape[3]
    train_flat = train_desc.reshape(levels * block_size, feature_width)
    queries = pred_desc[0]
    solved_list = []
    store = jnp.zeros((levels - 1, level_size, panel_rows, block_size), jnp.bfloat16)
    for level in range(levels):
        partial_rhs = rhs[level, 0]
        if level > 0:
            wanted = columns[level - 1, 0]
            which_level = wanted // level_size
            which_device = owner[which_level, wanted % level_size]
            picked = store[which_level, which_device]
            partial_rhs = partial_rhs - jnp.einsum(
                "krs,kst->rt", picked, off_blocks[level - 1, 0], preferred_element_type=jnp.float32
            )
        scaled = partial_rhs.astype(jnp.bfloat16)
        solved_level = jnp.dot(
            scaled, diag_inv[level, 0], preferred_element_type=jnp.float32
        ).astype(jnp.bfloat16)
        solved_list.append(solved_level)
        if level + 1 < levels:
            store = store.at[level].set(
                lax.all_gather(solved_level[None], "blk", axis=0, tiled=True)
            )
    own_panels = jnp.stack(solved_list)
    full_panels = lax.all_gather(own_panels, "grp", axis=1, tiled=True)
    own_rows = queries.shape[0] // level_size
    table = kernel_rows(queries, train_flat)
    table = table.reshape(own_rows * lax.axis_size("blk"), levels, block_size)
    predicted = lax.psum_scatter(
        jnp.einsum("pls,lrs->pr", table, full_panels, preferred_element_type=jnp.float32),
        "blk",
        scatter_dimension=0,
        tiled=True,
    )
    return (own_panels[:, None], predicted[None])


def solution(mesh):
    placed = (
        P(None, "blk", "grp", None),
        P(None, "blk", None, None),
        P(None, "blk", None, None, None),
        P(None, "blk", None),
        P(),
        P(None, "blk", None, None),
        P("grp", None, None),
    )
    return jax.shard_map(
        body,
        mesh=mesh,
        in_specs=placed,
        out_specs=(P(None, "blk", "grp", None), P("grp", "blk", None)),
        check_vma=False,
    )
```

profile of v0, /device:TPU:0, one launch (start us, length us, event | category | flops | bytes accessed | tf_op | source)
XLA Modules:
  0.0 219.0 jit_solution(18322663750539653613)
XLA Ops:
  7.2 0.0 copy-start
  7.2 0.0 reduce-scatter.2.cloned.1.call-start
  7.2 0.8 compare_select_fusion.13
  8.0 0.0 copy-start.5
  8.0 0.7 copy-done.5
  8.7 0.0 copy-start.1
  8.7 0.7 copy-done.1
  9.4 0.6 gather_fusion.4
  10.0 0.6 gather_fusion
  10.7 0.0 copy-start.3
  10.7 0.6 gather_fusion.2
  11.3 0.3 copy-done.3
  11.6 0.1 copy-done.4
  11.6 0.1 convolution_convert_fusion.3
  11.8 43.8 %all-gather = bf16[1024,128]{1,0:T(8,128)(2,1)S(1)} all-gather(bf16[64,128]{1,0:T(8,128)(2,1)S(1)} %convolution_convert_fusion.3), channel_id=2, replica_groups=mesh['blk'=16,'grp'=2] {'blk'}, dimensions={0}, use_global_device_ids=true | all-gather | bytes 278528 | tf_op jit(solution)/shard_map/all_gather | solution.py:43
  55.5 0.1 scatter.10
  55.7 0.6 gather_fusion.1
  56.3 0.3 copy-done.2
  56.5 0.3 convolution_convert_fusion.2
  56.8 36.8 %all-gather.1 = bf16[1024,128]{1,0:T(8,128)(2,1)S(1)} all-gather(bf16[64,128]{1,0:T(8,128)(2,1)S(1)} %convolution_convert_fusion.2), channel_id=3, replica_groups=mesh['blk'=16,'grp'=2] {'blk'}, dimensions={0}, use_global_device_ids=true | all-gather | bytes 278528 | tf_op jit(solution)/shard_map/all_gather | solution.py:43
  93.7 0.6 gather_fusion.3
  94.3 0.3 convolution_convert_fusion.1
  94.5 39.0 %all-gather.2 = bf16[1024,128]{1,0:T(8,128)(2,1)S(1)} all-gather(bf16[64,128]{1,0:T(8,128)(2,1)S(1)} %convolution_convert_fusion.1), channel_id=4, replica_groups=mesh['blk'=16,'grp'=2] {'blk'}, dimensions={0}, use_global_device_ids=true | all-gather | bytes 278528 | tf_op jit(solution)/shard_map/all_gather | solution.py:43
  133.5 0.6 gather_fusion.5
  134.1 0.3 fusion.8
  134.4 0.7 pad_maximum_fusion
  135.0 1.9 all_gather.15
  136.9 0.0 copy-done
  136.9 2.0 fusion.1
  138.9 1.0 convolution_bitcast_fusion
  139.9 0.0 reduce-scatter.2.cloned.1.call-update
  140.0 72.2 %reduce-scatter.2.cloned.1.call-done = f32[32,128]{1,0:T(8,128)} async-done(((f32[512,128]{1,0:T(8,128)}), f32[32,128]{1,0:T(8,128)}) %reduce-scatter.2.cloned.1.call-update) | async-done | bytes 16400 | tf_op jit(solution)/shard_map/reduce_scatter | solution.py:50
  (8 shorter events, 0.1 us)
Async XLA Ops:
  7.2 129.8 %copy-start = (bf16[4,1,128,1024]{3,2,1,0:T(8,128)(2,1)S(1)}, bf16[4,1,128,1024]{3,2,1,0:T(8,128)(2,1)}, u32[]{:S(2)}) copy-start(bf16[4,1,128,1024]{3,2,1,0:T(8,128)(2,1)} %param.18) | copy-start | bytes 3145732
  7.2 205.0 %reduce-scatter.2.cloned.1.call-start = ((), (), s32[]{:S(2)}) async-start(), calls=%async_computation.1 | async-start | bytes 278528 | tf_op jit(solution)/shard_map/reduce_scatter | solution.py:50
  8.0 0.7 copy-start.5
  8.7 0.7 copy-start.1
  10.7 0.9 copy-start.3
  10.7 1.0 copy-start.4
  55.5 1.0 copy-start.2
Sparse Core Ops, SparseCore 0:
  140.1 72.0 reduce-scatter.1
where the time goes:
time: 219 us
  blocking collectives  121 us (55%)
  waiting for transfers between devices  72.2 us (33%)
  between operations  14.1 us (6%)
  local copies, waits for them, and re-layouts  5.79 us (3%)
  matrix products  3.94 us (2%)
    all_gather x3, blocking collectives, body(): lax.all_gather(solved_level[None], 'blk', axis=0, tiled=True)  120 us
    reduce_scatter x1, waiting for transfers between devices, body(): lax.psum_scatter(jnp.einsum('pls,lrs->pr', table, full_panels, preferred_...  72.2 us
  transfers between devices with their start and end apart: 1, of which 1 were waited for; matrix products, arithmetic and copies ran while one was open for 0% of the time, Pallas kernels for 0%

commit v1 on v0

v1 whole, which is shorter than its diff:
```python
import functools

import jax
import jax.numpy as jnp
from jax import lax
from jax.experimental import pallas as pl
from jax.experimental.pallas import tpu as pltpu
from jax.sharding import PartitionSpec as P

F32 = jnp.float32
BF16 = jnp.bfloat16
CONTRACT_LAST = (((1,), (1,)), ((), ()))


def kernel(n, levels, columns_ref, owner_ref, rhs_ref, diag_ref, off_ref, train_hbm, pred_hbm,
           solved_ref, predicted_ref, *scratch):
    stores = scratch[: levels - 1]
    (full, train, pred, table, acc, outbox, inbox, pick_rows,
     local_sem, send_sem, recv_sem, pair_send, pair_recv, sum_send, sum_recv) = scratch[levels - 1:]
    me = lax.axis_index("blk")
    half = lax.axis_index("grp")
    rows, bs = rhs_ref.shape[1], rhs_ref.shape[2]
    width = train.shape[1]
    block_rows = outbox.shape[1]
    own_rows = predicted_ref.shape[0]

    load_train = pltpu.make_async_copy(train_hbm, train, local_sem.at[0])
    load_pred = pltpu.make_async_copy(pred_hbm, pred, local_sem.at[1])
    load_train.start()
    load_pred.start()

    barrier = pltpu.get_barrier_semaphore()

    def greet(step, carry):
        pl.semaphore_signal(barrier, inc=1, device_id={"blk": lax.rem(me + step, n)},
                            device_id_type=pl.DeviceIdType.MESH)
        return carry

    lax.fori_loop(1, n, greet, 0)
    pl.semaphore_signal(barrier, inc=1, device_id={"grp": 1 - half}, device_id_type=pl.DeviceIdType.MESH)

    def panel_copy(level, peer):
        return pltpu.make_async_remote_copy(
            src_ref=stores[level].at[me], dst_ref=stores[level].at[me],
            send_sem=send_sem.at[level], recv_sem=recv_sem.at[level],
            device_id={"blk": peer}, device_id_type=pl.DeviceIdType.MESH)

    def all_panels(level):
        every = stores[level].at[pl.ds(0, n - 1)]
        return pltpu.make_async_remote_copy(
            src_ref=every, dst_ref=every,
            send_sem=send_sem.at[level], recv_sem=recv_sem.at[level],
            device_id={"blk": lax.rem(me + 1, n)}, device_id_type=pl.DeviceIdType.MESH)

    def pair_copy(level):
        return pltpu.make_async_remote_copy(
            src_ref=full.at[level, half], dst_ref=full.at[level, half],
            send_sem=pair_send.at[level], recv_sem=pair_recv.at[level],
            device_id={"grp": 1 - half}, device_id_type=pl.DeviceIdType.MESH)

    def add_level(level):
        pair_copy(level).wait_recv()
        panel = full[level].reshape(2 * rows, bs)
        part = lax.dot_general(table[:, level * bs:(level + 1) * bs], panel, CONTRACT_LAST,
                               preferred_element_type=F32)
        part = part.reshape(acc.shape)
        acc[...] = part if level == 0 else acc[...] + part

    for level in range(levels):
        partial_rhs = rhs_ref[level]
        if level > 0:
            all_panels(level - 1).wait_recv()
            picks = []
            for k in range(columns_ref.shape[1]):
                wanted = columns_ref[level - 1, k]
                from_level = wanted // n
                place = owner_ref[from_level, lax.rem(wanted, n)]
                panel = stores[0][place]
                for other in range(1, level):
                    panel = jnp.where(from_level == other, stores[other][place], panel)
                picks.append(panel)
            partial_rhs = partial_rhs - jnp.dot(
                jnp.concatenate(picks, axis=1), off_ref[level - 1], preferred_element_type=F32)
        panel = jnp.dot(partial_rhs.astype(BF16), diag_ref[level], preferred_element_type=F32).astype(BF16)
        solved_ref[level] = panel
        full[level, half] = panel
        if level + 1 < levels:
            stores[level][me] = panel
        if level == 0:
            pl.semaphore_wait(barrier, n)
        if level + 1 < levels:

            def send_panel(step, carry):
                panel_copy(level, lax.rem(me + step, n)).start()
                return carry

            lax.fori_loop(1, n, send_panel, 0)
        pair_copy(level).start()
        if level == 0:
            load_train.wait()
            load_pred.wait()
            inner = lax.dot_general(pred[...], train[...], CONTRACT_LAST, preferred_element_type=F32)
            inner = inner / width
            table[...] = (inner * inner).astype(BF16)
        add_level(level)

    outbox[...] = acc[...].astype(BF16)

    def sum_copy(peer):
        return pltpu.make_async_remote_copy(
            src_ref=outbox.at[peer * own_rows // block_rows], dst_ref=inbox.at[me],
            send_sem=sum_send, recv_sem=sum_recv,
            device_id={"blk": peer}, device_id_type=pl.DeviceIdType.MESH)

    inbox[me] = jnp.zeros(inbox.shape[1:], BF16)

    def send_sum(step, carry):
        sum_copy(lax.rem(me + step, n)).start()
        return carry

    lax.fori_loop(1, n, send_sum, 0)
    every = inbox.at[pl.ds(0, n - 1)]
    sums = pltpu.make_async_remote_copy(
        src_ref=every, dst_ref=every, send_sem=sum_send, recv_sem=sum_recv,
        device_id={"blk": lax.rem(me + 1, n)}, device_id_type=pl.DeviceIdType.MESH)
    for level in range(levels):
        pair_copy(level).wait_send()
        if level + 1 < levels:
            all_panels(level).wait_send()
    sums.wait_recv()
    total = acc[me * own_rows // block_rows] + jnp.sum(inbox[...].astype(F32), axis=0)
    if own_rows == block_rows:
        predicted_ref[...] = total
    else:
        pick_rows[...] = total
        predicted_ref[...] = pick_rows[pl.ds(lax.rem(me * own_rows, block_rows), own_rows)]
    sums.wait_send()


def body(rhs, diag_inv, off_blocks, columns, owner, train_desc, pred_desc):
    levels, _, rows, bs = rhs.shape
    n = lax.axis_size("blk")
    kb = columns.shape[2]
    features = train_desc.shape[3]
    queries = pred_desc.shape[1]
    own_rows = queries // n
    block_rows = max(own_rows, 16)
    vmem = pl.BlockSpec(memory_space=pltpu.VMEM)
    smem = pl.BlockSpec(memory_space=pltpu.SMEM)
    hbm = pl.BlockSpec(memory_space=pl.ANY)
    solved, predicted = pl.pallas_call(
        functools.partial(kernel, n, levels),
        out_shape=(
            jax.ShapeDtypeStruct((levels, rows, bs), BF16),
            jax.ShapeDtypeStruct((own_rows, 2 * rows), F32),
        ),
        in_specs=[smem, smem, vmem, vmem, vmem, hbm, hbm],
        out_specs=(vmem, vmem),
        scratch_shapes=[pltpu.VMEM((n, rows, bs), BF16) for _ in range(levels - 1)] + [
            pltpu.VMEM((levels, 2, rows, bs), BF16),
            pltpu.VMEM((levels * bs, features), BF16),
            pltpu.VMEM((queries, features), BF16),
            pltpu.VMEM((queries, levels * bs), BF16),
            pltpu.VMEM((queries // block_rows, block_rows, 2 * rows), F32),
            pltpu.VMEM((queries // block_rows, block_rows, 2 * rows), BF16),
            pltpu.VMEM((n, block_rows, 2 * rows), BF16),
            pltpu.VMEM((block_rows, 2 * rows), F32),
            pltpu.SemaphoreType.DMA((2,)),
            pltpu.SemaphoreType.DMA((levels,)),
            pltpu.SemaphoreType.DMA((levels,)),
            pltpu.SemaphoreType.DMA((levels,)),
            pltpu.SemaphoreType.DMA((levels,)),
            pltpu.SemaphoreType.DMA,
            pltpu.SemaphoreType.DMA,
        ],
        compiler_params=pltpu.CompilerParams(
            collective_id=0, has_side_effects=True, vmem_limit_bytes=50 * 1024 * 1024),
    )(
        columns[:, 0], owner, rhs[:, 0], diag_inv[:, 0],
        off_blocks.reshape(levels - 1, kb * bs, bs),
        train_desc.reshape(levels * bs, features), pred_desc[0],
    )
    return solved[:, None], predicted[None]


def solution(mesh):
    placed = (
        P(None, "blk", "grp", None),
        P(None, "blk", None, None),
        P(None, "blk", None, None, None),
        P(None, "blk", None),
        P(),
        P(None, "blk", None, None),
        P("grp", None, None),
    )
    return jax.shard_map(
        body,
        mesh=mesh,
        in_specs=placed,
        out_specs=(P(None, "blk", "grp", None), P("grp", "blk", None)),
        check_vma=False,
    )
```

time: 219 us -> 44.2 us (0.20)
  blocking collectives: 121 us -> 0 us
  waiting for transfers between devices: 72.2 us -> 0 us
  Pallas kernels: 0 us -> 35.4 us
  between operations: 14.1 us -> 0.65 us
  matrix products: 3.94 us -> 0 us
    all_gather x4 -> x0, blocking collectives: 121 us -> none  [the longest x3 120 us: body(): lax.all_gather(solved_level[None], 'blk', axis=0, tiled=True)]
    reduce_scatter x1 -> x0, waiting for transfers between devices: 72.2 us -> none  [body(): lax.psum_scatter(jnp.einsum('pls,lrs->pr', table, full_panels, preferred_...]
    pallas_call x0 -> x1, Pallas kernels: none -> 35.4 us  [body(): pl.pallas_call(functools.partial(kernel, n, levels), out_shape=(jax.Shape...]
    unnamed x12 -> x17, local copies, waits for them, and re-layouts: 1.94 us -> 7.84 us
    dot_general x6 -> x0, matrix products: 3.94 us -> none  [the longest x1 1.97 us: kernel_rows(): lax.dot_general(queries, train_flat, (((1,), (1,)), ((), ())), preferred_...]
    gather x6 -> x0, local copies, waits for them, and re-layouts: 3.64 us -> none  [the longest x3 1.94 us: body(): which_device = owner[which_level, wanted % level_size]]
  transfers between devices with their start and end apart: 1 -> 0, of which waited for: 1 -> 0; matrix products, arithmetic and copies ran while one was open for 0% -> 0% of each run, Pallas kernels for 0% -> 0%
where the time goes in v1:
time: 44.2 us; the launch traced here: 43.9 us
  Pallas kernels  35.4 us (80%)
  local copies, waits for them, and re-layouts  7.84 us (18%)
  between operations  0.65 us (1%)
    pallas_call x1, Pallas kernels, body(): pl.pallas_call(functools.partial(kernel, n, levels), out_shape=(jax.Shape...  35.4 us
    unnamed x17, local copies, waits for them, and re-layouts  7.84 us

profile of v1, /device:TPU:0, one launch (start us, length us, event | category | flops | bytes accessed | tf_op | source)
XLA Modules:
  0.0 43.9 jit_solution(5703091577373314674)
XLA Ops:
  0.6 0.0 copy-start.6
  0.6 0.7 %copy-done.6 = s32[3,1,4]{2,1,0:T(1,128)S(1)} copy-done((s32[3,1,4]{2,1,0:T(1,128)S(1)}, s32[3,1,4]{2,1,0:T(1,128)}, u32[]{:S(2)}) %copy-start.6) | copy-done | bytes 72
  1.3 0.0 copy-start.5
  1.3 0.7 %copy-done.5 = s32[4,16]{1,0:T(4,128)S(1)} copy-done((s32[4,16]{1,0:T(4,128)S(1)}, s32[4,16]{1,0:T(4,128)}, u32[]{:S(2)}) %copy-start.5) | copy-done | bytes 280
  2.0 0.0 copy-start
  2.0 1.2 %copy-done = bf16[4,1,128,1024]{3,2,1,0:T(8,128)(2,1)S(1)} copy-done((bf16[4,1,128,1024]{3,2,1,0:T(8,128)(2,1)S(1)}, bf16[4,1,128,1024]{3,2,1,0:T(8,128)(2,1)}, u32[]{:S(2)}) %copy-start) | copy-done | bytes 1048600
  3.2 0.0 copy-start.1
  3.2 1.2 %copy-done.1 = bf16[1,512,1024]{2,1,0:T(8,128)(2,1)S(1)} copy-done((bf16[1,512,1024]{2,1,0:T(8,128)(2,1)S(1)}, bf16[1,512,1024]{2,1,0:T(8,128)(2,1)}, u32[]{:S(2)}) %copy-start.1) | copy-done | bytes 1048600
  4.4 0.0 copy-start.2
  4.4 1.0 %copy-done.2 = bf16[3,1,4,128,128]{4,3,2,1,0:T(8,128)(2,1)S(1)} copy-done((bf16[3,1,4,128,128]{4,3,2,1,0:T(8,128)(2,1)S(1)}, bf16[3,1,4,128,128]{4,3,2,1,0:T(8,128)(2,1)}, u32[]{:S(2)}) %copy-start.2) | copy-done | bytes 393240
  5.4 0.0 copy-start.3
  5.4 0.9 %copy-done.3 = f32[4,1,64,128]{3,2,1,0:T(8,128)S(1)} copy-done((f32[4,1,64,128]{3,2,1,0:T(8,128)S(1)}, f32[4,1,64,128]{3,2,1,0:T(8,128)}, u32[]{:S(2)}) %copy-start.3) | copy-done | bytes 131096
  6.3 0.0 copy-start.4
  6.3 0.9 %copy-done.4 = bf16[4,1,128,128]{3,2,1,0:T(8,128)(2,1)S(1)} copy-done((bf16[4,1,128,128]{3,2,1,0:T(8,128)(2,1)S(1)}, bf16[4,1,128,128]{3,2,1,0:T(8,128)(2,1)}, u32[]{:S(2)}) %copy-start.4) | copy-done | bytes 131096
  7.2 35.4 %shard_map.86 = (bf16[4,64,128]{2,1,0:T(8,128)(2,1)S(1)}, f32[32,128]{1,0:T(8,128)S(1)}) custom-call(s32[3,4]{1,0:T(4,128)S(1)} %bitcast.19, s32[4,16]{1,0:T(4,128)S(1)} %copy-done.5, f32[4,64,128]{2,1,0:T(8,128)S(1)} %bitcast.15, bf16[4,128,128]{2,1,0:T(8,128)(2,1)S(1)} %bitcast.16, bf16[3,512,128]{2,1,0:T(8,128)(2,1)S(1)} %bitcast.14, ...), custom_call_target="tpu_custom_call" | custom-call | tf_op jit(solution)/shard_map/pallas_call | solution.py:151
  42.7 0.6 %copy.15 = bf16[4,1,64,128]{3,2,1,0:T(8,128)(2,1)} copy(bf16[4,1,64,128]{3,2,1,0:T(8,128)(2,1)S(1)} %bitcast.17) | data formatting | bytes 131072
  43.3 0.6 %copy.16 = f32[1,32,128]{2,1,0:T(8,128)} copy(f32[1,32,128]{2,1,0:T(8,128)S(1)} %bitcast.18) | data formatting | bytes 32768
  (1 shorter events, 0.0 us)
Async XLA Ops:
  0.6 0.7 %copy-start.6 = (s32[3,1,4]{2,1,0:T(1,128)S(1)}, s32[3,1,4]{2,1,0:T(1,128)}, u32[]{:S(2)}) copy-start(s32[3,1,4]{2,1,0:T(1,128)} %param.10) | copy-start | bytes 148
  1.3 0.7 %copy-start.5 = (s32[4,16]{1,0:T(4,128)S(1)}, s32[4,16]{1,0:T(4,128)}, u32[]{:S(2)}) copy-start(s32[4,16]{1,0:T(4,128)} %owner_ref.1) | copy-start | bytes 772
  2.0 1.2 %copy-start = (bf16[4,1,128,1024]{3,2,1,0:T(8,128)(2,1)S(1)}, bf16[4,1,128,1024]{3,2,1,0:T(8,128)(2,1)}, u32[]{:S(2)}) copy-start(bf16[4,1,128,1024]{3,2,1,0:T(8,128)(2,1)} %param.12) | copy-start | bytes 3145732
  3.2 1.2 %copy-start.1 = (bf16[1,512,1024]{2,1,0:T(8,128)(2,1)S(1)}, bf16[1,512,1024]{2,1,0:T(8,128)(2,1)}, u32[]{:S(2)}) copy-start(bf16[1,512,1024]{2,1,0:T(8,128)(2,1)} %param.13) | copy-start | bytes 3145732
  4.4 1.0 %copy-start.2 = (bf16[3,1,4,128,128]{4,3,2,1,0:T(8,128)(2,1)S(1)}, bf16[3,1,4,128,128]{4,3,2,1,0:T(8,128)(2,1)}, u32[]{:S(2)}) copy-start(bf16[3,1,4,128,128]{4,3,2,1,0:T(8,128)(2,1)} %param.9) | copy-start | bytes 1179652
  5.4 0.9 %copy-start.3 = (f32[4,1,64,128]{3,2,1,0:T(8,128)S(1)}, f32[4,1,64,128]{3,2,1,0:T(8,128)}, u32[]{:S(2)}) copy-start(f32[4,1,64,128]{3,2,1,0:T(8,128)} %param.7) | copy-start | bytes 393220
  6.3 0.9 %copy-start.4 = (bf16[4,1,128,128]{3,2,1,0:T(8,128)(2,1)S(1)}, bf16[4,1,128,128]{3,2,1,0:T(8,128)(2,1)}, u32[]{:S(2)}) copy-start(bf16[4,1,128,128]{3,2,1,0:T(8,128)(2,1)} %param.8) | copy-start | bytes 393220

commit v2 on v1

--- a/solution.py
+++ b/solution.py
@@ -12,22 +12,25 @@
 CONTRACT_LAST = (((1,), (1,)), ((), ()))
 
 
-def kernel(n, levels, columns_ref, owner_ref, rhs_ref, diag_ref, off_ref, train_hbm, pred_hbm,
-           solved_ref, predicted_ref, *scratch):
+def kernel(n, levels, *refs):
+    operands, (solved_ref, predicted_ref), scratch = refs[:7], refs[7:9], refs[9:]
     stores = scratch[: levels - 1]
-    (full, train, pred, table, acc, outbox, inbox, pick_rows,
+    (rhs_ref, diag_ref, columns_ref, owner_ref, off_ref, pred, train,
+     full, table, acc, outbox, inbox, pick_rows,
      local_sem, send_sem, recv_sem, pair_send, pair_recv, sum_send, sum_recv) = scratch[levels - 1:]
     me = lax.axis_index("blk")
     half = lax.axis_index("grp")
-    rows, bs = rhs_ref.shape[1], rhs_ref.shape[2]
+    rows, bs = rhs_ref.shape[2], rhs_ref.shape[3]
     width = train.shape[1]
+    kb = columns_ref.shape[2]
     block_rows = outbox.shape[1]
-    own_rows = predicted_ref.shape[0]
-
-    load_train = pltpu.make_async_copy(train_hbm, train, local_sem.at[0])
-    load_pred = pltpu.make_async_copy(pred_hbm, pred, local_sem.at[1])
-    load_train.start()
-    load_pred.start()
+    own_rows = predicted_ref.shape[1]
+
+    here = (rhs_ref, diag_ref, columns_ref, owner_ref, off_ref, pred, train)
+    loads = [pltpu.make_async_copy(operand, local, local_sem.at[i])
+             for i, (operand, local) in enumerate(zip(operands, here))]
+    for load in loads:
+        load.start()
 
     barrier = pltpu.get_barrier_semaphore()
 
@@ -67,12 +70,15 @@
         acc[...] = part if level == 0 else acc[...] + part
 
     for level in range(levels):
-        partial_rhs = rhs_ref[level]
+        if level == 0:
+            loads[0].wait()
+            loads[1].wait()
+        partial_rhs = rhs_ref[level, 0]
         if level > 0:
             all_panels(level - 1).wait_recv()
             picks = []
-            for k in range(columns_ref.shape[1]):
-                wanted = columns_ref[level - 1, k]
+            for k in range(kb):
+                wanted = columns_ref[level - 1, 0, k]
                 from_level = wanted // n
                 place = owner_ref[from_level, lax.rem(wanted, n)]
                 panel = stores[0][place]
@@ -80,9 +86,9 @@
                     panel = jnp.where(from_level == other, stores[other][place], panel)
                 picks.append(panel)
             partial_rhs = partial_rhs - jnp.dot(
-                jnp.concatenate(picks, axis=1), off_ref[level - 1], preferred_element_type=F32)
-        panel = jnp.dot(partial_rhs.astype(BF16), diag_ref[level], preferred_element_type=F32).astype(BF16)
-        solved_ref[level] = panel
+                jnp.concatenate(picks, axis=1), off_ref[level - 1, 0].reshape(kb * bs, bs), preferred_element_type=F32)
+        panel = jnp.dot(partial_rhs.astype(BF16), diag_ref[level, 0], preferred_element_type=F32).astype(BF16)
+        solved_ref[level, 0] = panel
         full[level, half] = panel
         if level + 1 < levels:
             stores[level][me] = panel
@@ -97,8 +103,8 @@
             lax.fori_loop(1, n, send_panel, 0)
         pair_copy(level).start()
         if level == 0:
-            load_train.wait()
-            load_pred.wait()
+            for load in loads[2:]:
+                load.wait()
             inner = lax.dot_general(pred[...], train[...], CONTRACT_LAST, preferred_element_type=F32)
             inner = inner / width
             table[...] = (inner * inner).astype(BF16)
@@ -130,42 +136,45 @@
     sums.wait_recv()
     total = acc[me * own_rows // block_rows] + jnp.sum(inbox[...].astype(F32), axis=0)
     if own_rows == block_rows:
-        predicted_ref[...] = total
+        predicted_ref[0] = total
     else:
         pick_rows[...] = total
-        predicted_ref[...] = pick_rows[pl.ds(lax.rem(me * own_rows, block_rows), own_rows)]
+        predicted_ref[0] = pick_rows[pl.ds(lax.rem(me * own_rows, block_rows), own_rows)]
     sums.wait_send()
 
 
 def body(rhs, diag_inv, off_blocks, columns, owner, train_desc, pred_desc):
     levels, _, rows, bs = rhs.shape
     n = lax.axis_size("blk")
-    kb = columns.shape[2]
     features = train_desc.shape[3]
     queries = pred_desc.shape[1]
     own_rows = queries // n
     block_rows = max(own_rows, 16)
     vmem = pl.BlockSpec(memory_space=pltpu.VMEM)
-    smem = pl.BlockSpec(memory_space=pltpu.SMEM)
-    hbm = pl.BlockSpec(memory_space=pl.ANY)
+    hbm = pl.BlockSpec(memory_space=pltpu.HBM)
     solved, predicted = pl.pallas_call(
         functools.partial(kernel, n, levels),
         out_shape=(
-            jax.ShapeDtypeStruct((levels, rows, bs), BF16),
-            jax.ShapeDtypeStruct((own_rows, 2 * rows), F32),
+            jax.ShapeDtypeStruct((levels, 1, rows, bs), BF16),
+            jax.ShapeDtypeStruct((1, own_rows, 2 * rows), F32),
         ),
-        in_specs=[smem, smem, vmem, vmem, vmem, hbm, hbm],
+        in_specs=[hbm] * 7,
         out_specs=(vmem, vmem),
         scratch_shapes=[pltpu.VMEM((n, rows, bs), BF16) for _ in range(levels - 1)] + [
+            pltpu.VMEM(rhs.shape, F32),
+            pltpu.VMEM(diag_inv.shape, BF16),
+            pltpu.SMEM(columns.shape, jnp.int32),
+            pltpu.SMEM(owner.shape, jnp.int32),
+            pltpu.VMEM(off_blocks.shape, BF16),
+            pltpu.VMEM((queries, features), BF16),
+            pltpu.VMEM((levels * bs, features), BF16),
             pltpu.VMEM((levels, 2, rows, bs), BF16),
-            pltpu.VMEM((levels * bs, features), BF16),
-            pltpu.VMEM((queries, features), BF16),
             pltpu.VMEM((queries, levels * bs), BF16),
             pltpu.VMEM((queries // block_rows, block_rows, 2 * rows), F32),
             pltpu.VMEM((queries // block_rows, block_rows, 2 * rows), BF16),
             pltpu.VMEM((n, block_rows, 2 * rows), BF16),
             pltpu.VMEM((block_rows, 2 * rows), F32),
-            pltpu.SemaphoreType.DMA((2,)),
+            pltpu.SemaphoreType.DMA((7,)),
             pltpu.SemaphoreType.DMA((levels,)),
             pltpu.SemaphoreType.DMA((levels,)),
             pltpu.SemaphoreType.DMA((levels,)),
@@ -174,13 +183,12 @@
             pltpu.SemaphoreType.DMA,
         ],
         compiler_params=pltpu.CompilerParams(
-            collective_id=0, has_side_effects=True, vmem_limit_bytes=50 * 1024 * 1024),
+            collective_id=0, has_side_effects=True, vmem_limit_bytes=65000 * 1024),
     )(
-        columns[:, 0], owner, rhs[:, 0], diag_inv[:, 0],
-        off_blocks.reshape(levels - 1, kb * bs, bs),
-        train_desc.reshape(levels * bs, features), pred_desc[0],
+        rhs, diag_inv, columns, owner, off_blocks, pred_desc[0],
+        train_desc.reshape(levels * bs, features),
     )
-    return solved[:, None], predicted[None]
+    return solved, predicted
 
 
 def solution(mesh):

time: 44.2 us -> 38.3 us (0.87)
  local copies, waits for them, and re-layouts: 7.84 us -> 2.09 us
    unnamed x17 -> x4, local copies, waits for them, and re-layouts: 7.84 us -> 2.09 us
where the time goes in v2:
time: 38.3 us; the launch traced here: 38.1 us
  Pallas kernels  35.4 us (92%)
  local copies, waits for them, and re-layouts  2.09 us (5%)
  between operations  0.65 us (2%)
    pallas_call x1, Pallas kernels, body(): pl.pallas_call(functools.partial(kernel, n, levels), out_shape=(jax.Shape...  35.4 us
    unnamed x4, local copies, waits for them, and re-layouts  2.09 us

profile of v2, /device:TPU:0, one launch (start us, length us, event | category | flops | bytes accessed | tf_op | source)
XLA Modules:
  0.0 38.1 jit_solution(13650070905095741461)
XLA Ops:
  0.6 35.4 %shard_map.86 = (bf16[4,1,64,128]{3,2,1,0:T(8,128)(2,1)}, f32[1,32,128]{2,1,0:T(8,128)}) custom-call(f32[4,1,64,128]{3,2,1,0:T(8,128)} %refs_0_.1, bf16[4,1,128,128]{3,2,1,0:T(8,128)(2,1)} %refs_1_.1, s32[3,1,4]{2,1,0:T(1,128)} %refs_2_.1, s32[4,16]{1,0:T(4,128)} %refs_3_.1, bf16[3,1,4,128,128]{4,3,2,1,0:T(8,128)(2,1)} %refs_4_.1, ...), custom_call_target="tpu_custom_call" | custom-call | tf_op jit(solution)/shard_map/pallas_call | solution.py:155
  36.0 0.0 copy-start
  36.0 1.5 %copy.11 = bf16[4,1,64,128]{3,2,1,0:T(8,128)(2,1)} copy(bf16[4,1,64,128]{3,2,1,0:T(8,128)(2,1)} %get-tuple-element.4) | data formatting | bytes 131072
  37.5 0.0 copy-done
  37.5 0.6 %copy.12 = f32[1,32,128]{2,1,0:T(8,128)} copy(f32[1,32,128]{2,1,0:T(8,128)S(1)} %copy-done) | data formatting | bytes 32768
Async XLA Ops:
  36.0 1.5 %copy-start = (f32[1,32,128]{2,1,0:T(8,128)S(1)}, f32[1,32,128]{2,1,0:T(8,128)}, u32[]{:S(2)}) copy-start(f32[1,32,128]{2,1,0:T(8,128)} %get-tuple-element.5) | copy-start | bytes 49156

commit v3 on v2

--- a/solution.py
+++ b/solution.py
@@ -12,12 +12,12 @@
 CONTRACT_LAST = (((1,), (1,)), ((), ()))
 
 
-def kernel(n, levels, *refs):
+def kernel(n, plane, levels, *refs):
     operands, (solved_ref, predicted_ref), scratch = refs[:7], refs[7:9], refs[9:]
     stores = scratch[: levels - 1]
     (rhs_ref, diag_ref, columns_ref, owner_ref, off_ref, pred, train,
      full, table, acc, outbox, inbox, pick_rows,
-     local_sem, send_sem, recv_sem, pair_send, pair_recv, sum_send, sum_recv) = scratch[levels - 1:]
+     local_sem, send_sem, recv_sem, line_send, line_recv, pair_send, pair_recv, sum_send, sum_recv) = scratch[levels - 1:]
     me = lax.axis_index("blk")
     half = lax.axis_index("grp")
     rows, bs = rhs_ref.shape[2], rhs_ref.shape[3]
@@ -42,18 +42,36 @@
     lax.fori_loop(1, n, greet, 0)
     pl.semaphore_signal(barrier, inc=1, device_id={"grp": 1 - half}, device_id_type=pl.DeviceIdType.MESH)
 
-    def panel_copy(level, peer):
-        return pltpu.make_async_remote_copy(
-            src_ref=stores[level].at[me], dst_ref=stores[level].at[me],
-            send_sem=send_sem.at[level], recv_sem=recv_sem.at[level],
-            device_id={"blk": peer}, device_id_type=pl.DeviceIdType.MESH)
+    line, spot = me // plane, lax.rem(me, plane)
+    lines = n // plane
+
+    def on_line(step):
+        return lax.rem(line + step, lines) * plane + spot
+
+    def in_plane(step):
+        return line * plane + lax.rem(spot + step, plane)
+
+    def panel_copy(level, block, peer, send, recv):
+        return pltpu.make_async_remote_copy(
+            src_ref=stores[level].at[block], dst_ref=stores[level].at[block],
+            send_sem=send, recv_sem=recv, device_id={"blk": peer}, device_id_type=pl.DeviceIdType.MESH)
+
+    def line_copy(level, step):
+        return panel_copy(level, me, on_line(step), line_send.at[level, step], line_recv.at[level, step])
+
+    def share(level, block):
+        def send(step, carry):
+            panel_copy(level, block, in_plane(step), send_sem.at[level], recv_sem.at[level]).start()
+            return carry
+
+        lax.fori_loop(1, plane, send, 0)
 
     def all_panels(level):
-        every = stores[level].at[pl.ds(0, n - 1)]
+        every = stores[level].at[pl.ds(0, n - lines)]
         return pltpu.make_async_remote_copy(
             src_ref=every, dst_ref=every,
             send_sem=send_sem.at[level], recv_sem=recv_sem.at[level],
-            device_id={"blk": lax.rem(me + 1, n)}, device_id_type=pl.DeviceIdType.MESH)
+            device_id={"blk": in_plane(1)}, device_id_type=pl.DeviceIdType.MESH)
 
     def pair_copy(level):
         return pltpu.make_async_remote_copy(
@@ -95,13 +113,14 @@
         if level == 0:
             pl.semaphore_wait(barrier, n)
         if level + 1 < levels:
-
-            def send_panel(step, carry):
-                panel_copy(level, lax.rem(me + step, n)).start()
-                return carry
-
-            lax.fori_loop(1, n, send_panel, 0)
+            for step in range(1, lines):
+                line_copy(level, step).start()
+            share(level, me)
         pair_copy(level).start()
+        if level + 1 < levels:
+            for step in range(1, lines):
+                line_copy(level, step).wait_recv()
+                share(level, on_line(lines - step))
         if level == 0:
             for load in loads[2:]:
                 load.wait()
@@ -133,6 +152,8 @@
         pair_copy(level).wait_send()
         if level + 1 < levels:
             all_panels(level).wait_send()
+            for step in range(1, lines):
+                line_copy(level, step).wait_send()
     sums.wait_recv()
     total = acc[me * own_rows // block_rows] + jnp.sum(inbox[...].astype(F32), axis=0)
     if own_rows == block_rows:
@@ -143,9 +164,17 @@
     sums.wait_send()
 
 
+def plane_of(n):
+    plane = 1
+    while plane * plane < n:
+        plane *= 2
+    return plane if n % plane == 0 else n
+
+
 def body(rhs, diag_inv, off_blocks, columns, owner, train_desc, pred_desc):
     levels, _, rows, bs = rhs.shape
     n = lax.axis_size("blk")
+    plane = plane_of(n)
     features = train_desc.shape[3]
     queries = pred_desc.shape[1]
     own_rows = queries // n
@@ -153,7 +182,7 @@
     vmem = pl.BlockSpec(memory_space=pltpu.VMEM)
     hbm = pl.BlockSpec(memory_space=pltpu.HBM)
     solved, predicted = pl.pallas_call(
-        functools.partial(kernel, n, levels),
+        functools.partial(kernel, n, plane, levels),
         out_shape=(
             jax.ShapeDtypeStruct((levels, 1, rows, bs), BF16),
             jax.ShapeDtypeStruct((1, own_rows, 2 * rows), F32),
@@ -177,6 +206,8 @@
             pltpu.SemaphoreType.DMA((7,)),
             pltpu.SemaphoreType.DMA((levels,)),
             pltpu.SemaphoreType.DMA((levels,)),
+            pltpu.SemaphoreType.DMA((levels, n // plane)),
+            pltpu.SemaphoreType.DMA((levels, n // plane)),
             pltpu.SemaphoreType.DMA((levels,)),
             pltpu.SemaphoreType.DMA((levels,)),
             pltpu.SemaphoreType.DMA,

time: 38.3 us -> 38.9 us (1.016)
  Pallas kernels: 35.4 us -> 36 us
    pallas_call x1, Pallas kernels: 35.4 us -> 36 us  [body(): pl.pallas_call(functools.partial(kernel, n, plane, levels), out_shape=(ja...]
where the time goes in v3:
time: 38.9 us; the launch traced here: 38.7 us
  Pallas kernels  36 us (93%)
  local copies, waits for them, and re-layouts  2.09 us (5%)
  between operations  0.65 us (2%)
    pallas_call x1, Pallas kernels, body(): pl.pallas_call(functools.partial(kernel, n, plane, levels), out_shape=(ja...  36 us
    unnamed x4, local copies, waits for them, and re-layouts  2.09 us

profile of v3, /device:TPU:0, one launch (start us, length us, event | category | flops | bytes accessed | tf_op | source)
XLA Modules:
  0.0 38.7 jit_solution(7833563511433084247)
XLA Ops:
  0.6 36.0 %shard_map.86 = (bf16[4,1,64,128]{3,2,1,0:T(8,128)(2,1)}, f32[1,32,128]{2,1,0:T(8,128)}) custom-call(f32[4,1,64,128]{3,2,1,0:T(8,128)} %refs_0_.1, bf16[4,1,128,128]{3,2,1,0:T(8,128)(2,1)} %refs_1_.1, s32[3,1,4]{2,1,0:T(1,128)} %refs_2_.1, s32[4,16]{1,0:T(4,128)} %refs_3_.1, bf16[3,1,4,128,128]{4,3,2,1,0:T(8,128)(2,1)} %refs_4_.1, ...), custom_call_target="tpu_custom_call" | custom-call | tf_op jit(solution)/shard_map/pallas_call | solution.py:184
  36.6 0.0 copy-start
  36.6 1.5 %copy.11 = bf16[4,1,64,128]{3,2,1,0:T(8,128)(2,1)} copy(bf16[4,1,64,128]{3,2,1,0:T(8,128)(2,1)} %get-tuple-element.4) | data formatting | bytes 131072
  38.1 0.0 copy-done
  38.1 0.6 %copy.12 = f32[1,32,128]{2,1,0:T(8,128)} copy(f32[1,32,128]{2,1,0:T(8,128)S(1)} %copy-done) | data formatting | bytes 32768
Async XLA Ops:
  36.6 1.5 %copy-start = (f32[1,32,128]{2,1,0:T(8,128)S(1)}, f32[1,32,128]{2,1,0:T(8,128)}, u32[]{:S(2)}) copy-start(f32[1,32,128]{2,1,0:T(8,128)} %get-tuple-element.5) | copy-start | bytes 49156

commit v4 on v2

--- a/solution.py
+++ b/solution.py
@@ -33,6 +33,8 @@
         load.start()
 
     barrier = pltpu.get_barrier_semaphore()
+
+    stride = 7 if n % 7 else 1
 
     def greet(step, carry):
         pl.semaphore_signal(barrier, inc=1, device_id={"blk": lax.rem(me + step, n)},
@@ -97,7 +99,7 @@
         if level + 1 < levels:
 
             def send_panel(step, carry):
-                panel_copy(level, lax.rem(me + step, n)).start()
+                panel_copy(level, lax.rem(me + step * stride, n)).start()
                 return carry
 
             lax.fori_loop(1, n, send_panel, 0)
@@ -121,7 +123,7 @@
     inbox[me] = jnp.zeros(inbox.shape[1:], BF16)
 
     def send_sum(step, carry):
-        sum_copy(lax.rem(me + step, n)).start()
+        sum_copy(lax.rem(me + step * stride, n)).start()
         return carry
 
     lax.fori_loop(1, n, send_sum, 0)
@@ -141,6 +143,15 @@
         pick_rows[...] = total
         predicted_ref[0] = pick_rows[pl.ds(lax.rem(me * own_rows, block_rows), own_rows)]
     sums.wait_send()
+
+
+def store_results(solved_in, predicted_in, solved_out, predicted_out, sem):
+    first = pltpu.make_async_copy(solved_in, solved_out, sem.at[0])
+    second = pltpu.make_async_copy(predicted_in, predicted_out, sem.at[1])
+    first.start()
+    second.start()
+    first.wait()
+    second.wait()
 
 
 def body(rhs, diag_inv, off_blocks, columns, owner, train_desc, pred_desc):
@@ -188,7 +199,13 @@
         rhs, diag_inv, columns, owner, off_blocks, pred_desc[0],
         train_desc.reshape(levels * bs, features),
     )
-    return solved, predicted
+    return pl.pallas_call(
+        store_results,
+        out_shape=(jax.ShapeDtypeStruct(solved.shape, BF16), jax.ShapeDtypeStruct(predicted.shape, F32)),
+        in_specs=[vmem, vmem],
+        out_specs=(hbm, hbm),
+        scratch_shapes=[pltpu.SemaphoreType.DMA((2,))],
+    )(solved, predicted)
 
 
 def solution(mesh):

time: 38.3 us -> 36.6 us (0.956)
  local copies, waits for them, and re-layouts: 2.09 us -> 0 us
    unnamed x4 -> x0, local copies, waits for them, and re-layouts: 2.09 us -> none
    pallas_call x0 -> x1, Pallas kernels: none -> 1.49 us  [body(): pl.pallas_call(store_results, out_shape=(jax.ShapeDtypeStruct(solved.shap...]
    pallas_call x1, Pallas kernels: 35.4 us -> 34.2 us  [body(): pl.pallas_call(functools.partial(kernel, n, levels), out_shape=(jax.Shape...]
where the time goes in v4:
time: 36.6 us; the launch traced here: 36.4 us
  Pallas kernels  35.7 us (98%)
  between operations  0.64 us (2%)
    pallas_call x1, Pallas kernels, body(): pl.pallas_call(functools.partial(kernel, n, levels), out_shape=(jax.Shape...  34.2 us
    pallas_call x1, Pallas kernels, body(): pl.pallas_call(store_results, out_shape=(jax.ShapeDtypeStruct(solved.shap...  1.49 us

profile of v4, /device:TPU:0, one launch (start us, length us, event | category | flops | bytes accessed | tf_op | source)
XLA Modules:
  0.0 36.4 jit_solution(14571988539801904052)
XLA Ops:
  0.6 34.2 %shard_map.86 = (bf16[4,1,64,128]{3,2,1,0:T(8,128)(2,1)}, f32[1,32,128]{2,1,0:T(8,128)}) custom-call(f32[4,1,64,128]{3,2,1,0:T(8,128)} %refs_0_.1, bf16[4,1,128,128]{3,2,1,0:T(8,128)(2,1)} %refs_1_.1, s32[3,1,4]{2,1,0:T(1,128)} %refs_2_.1, s32[4,16]{1,0:T(4,128)} %refs_3_.1, bf16[3,1,4,128,128]{4,3,2,1,0:T(8,128)(2,1)} %refs_4_.1, ...), custom_call_target="tpu_custom_call" | custom-call | tf_op jit(solution)/shard_map/pallas_call | solution.py:166
  34.9 1.5 %shard_map.87 = (bf16[4,1,64,128]{3,2,1,0:T(8,128)(2,1)}, f32[1,32,128]{2,1,0:T(8,128)}) custom-call(bf16[4,1,64,128]{3,2,1,0:T(8,128)(2,1)} %get-tuple-element.4.solved_in, f32[1,32,128]{2,1,0:T(8,128)} %get-tuple-element.5.predicted_in), custom_call_target="tpu_custom_call" | custom-call | tf_op jit(solution)/shard_map/pallas_call | solution.py:202

commit v5 on v4

--- a/solution.py
+++ b/solution.py
@@ -35,6 +35,10 @@
     barrier = pltpu.get_barrier_semaphore()
 
     stride = 7 if n % 7 else 1
+
+    def peer_at(offset):
+        return (lax.rem(me // 4 + offset // 4, n // 4) * 4 + lax.rem(lax.rem(me, 4) // 2 + lax.rem(offset, 4) // 2, 2) * 2
+                + lax.rem(me + offset, 2))
 
     def greet(step, carry):
         pl.semaphore_signal(barrier, inc=1, device_id={"blk": lax.rem(me + step, n)},
@@ -99,7 +103,7 @@
         if level + 1 < levels:
 
             def send_panel(step, carry):
-                panel_copy(level, lax.rem(me + step * stride, n)).start()
+                panel_copy(level, peer_at(lax.rem(step * stride, n))).start()
                 return carry
 
             lax.fori_loop(1, n, send_panel, 0)
@@ -123,7 +127,7 @@
     inbox[me] = jnp.zeros(inbox.shape[1:], BF16)
 
     def send_sum(step, carry):
-        sum_copy(lax.rem(me + step * stride, n)).start()
+        sum_copy(peer_at(lax.rem(step * stride, n))).start()
         return carry
 
     lax.fori_loop(1, n, send_sum, 0)
@@ -131,10 +135,6 @@
     sums = pltpu.make_async_remote_copy(
         src_ref=every, dst_ref=every, send_sem=sum_send, recv_sem=sum_recv,
         device_id={"blk": lax.rem(me + 1, n)}, device_id_type=pl.DeviceIdType.MESH)
-    for level in range(levels):
-        pair_copy(level).wait_send()
-        if level + 1 < levels:
-            all_panels(level).wait_send()
     sums.wait_recv()
     total = acc[me * own_rows // block_rows] + jnp.sum(inbox[...].astype(F32), axis=0)
     if own_rows == block_rows:
@@ -142,6 +142,10 @@
     else:
         pick_rows[...] = total
         predicted_ref[0] = pick_rows[pl.ds(lax.rem(me * own_rows, block_rows), own_rows)]
+    for level in range(levels):
+        pair_copy(level).wait_send()
+        if level + 1 < levels:
+            all_panels(level).wait_send()
     sums.wait_send()
 
 

time: 36.6 us -> 36.2 us (0.989)
  Pallas kernels: 35.7 us -> 35.2 us
    pallas_call x1, Pallas kernels: 34.2 us -> 33.7 us  [body(): pl.pallas_call(functools.partial(kernel, n, levels), out_shape=(jax.Shape...]
where the time goes in v5:
time: 36.2 us; the launch traced here: 35.9 us
  Pallas kernels  35.2 us (97%)
  between operations  0.64 us (2%)
    pallas_call x1, Pallas kernels, body(): pl.pallas_call(functools.partial(kernel, n, levels), out_shape=(jax.Shape...  33.7 us
    pallas_call x1, Pallas kernels, body(): pl.pallas_call(store_results, out_shape=(jax.ShapeDtypeStruct(solved.shap...  1.49 us

profile of v5, /device:TPU:0, one launch (start us, length us, event | category | flops | bytes accessed | tf_op | source)
XLA Modules:
  0.0 35.9 jit_solution(3943537687108132625)
XLA Ops:
  0.6 33.7 %shard_map.86 = (bf16[4,1,64,128]{3,2,1,0:T(8,128)(2,1)}, f32[1,32,128]{2,1,0:T(8,128)}) custom-call(f32[4,1,64,128]{3,2,1,0:T(8,128)} %refs_0_.1, bf16[4,1,128,128]{3,2,1,0:T(8,128)(2,1)} %refs_1_.1, s32[3,1,4]{2,1,0:T(1,128)} %refs_2_.1, s32[4,16]{1,0:T(4,128)} %refs_3_.1, bf16[3,1,4,128,128]{4,3,2,1,0:T(8,128)(2,1)} %refs_4_.1, ...), custom_call_target="tpu_custom_call" | custom-call | tf_op jit(solution)/shard_map/pallas_call | solution.py:170
  34.4 1.5 %shard_map.87 = (bf16[4,1,64,128]{3,2,1,0:T(8,128)(2,1)}, f32[1,32,128]{2,1,0:T(8,128)}) custom-call(bf16[4,1,64,128]{3,2,1,0:T(8,128)(2,1)} %get-tuple-element.4.solved_in, f32[1,32,128]{2,1,0:T(8,128)} %get-tuple-element.5.predicted_in), custom_call_target="tpu_custom_call" | custom-call | tf_op jit(solution)/shard_map/pallas_call | solution.py:206
